TPU v7x, 256 devices: a whole 4x4x8 slice. The times are simulated.
256 devices in a mesh: blk: 128 (over y, x_hi, z, core), col: 2 (over x_lo).
Axes of the slice: x: 4 (x_hi: 2, x_lo: 2; x = x_hi * 2 + x_lo), y: 4, z: 8, core: 2. Of those that a mesh axis runs over, the one named last changes fastest.
Arguments:
- features: bfloat16 [131072, 256], P('blk', 'col'), may hold values from -6 to 6
- tile_values: bfloat16 [36864, 128, 128], P('blk'), may hold values from -0.09375 to 0.09375
- tile_index: int32 [3, 36864], P(None, 'blk'), may hold values from 0 to 127, as said below
- send_rows: int32 [128, 128, 8], P('blk'), may hold values from 0 to 1023
- slot_counts: int32 [128, 128], P('blk'), may hold values from 0 to 8, as said below
- far_weight: bfloat16 [131072, 1024], P('blk'), may hold values from -0.1875 to 0.1875
- weight_one: bfloat16 [256, 256], replicated, may hold values from -0.375 to 0.375
- weight_two: bfloat16 [256, 256], replicated, may hold values from -0.375 to 0.375
Outputs:
- node_output: bfloat16 [131072, 256], P('blk', 'col')
Inputs may be any that keep to these rules, and one draw needn't show every extreme that they name: tile_index[0, t] is a partition at most 4 steps from t // 288 around the closed cycle of 128 partitions, and every cycle offset from -4 to 4 occurs among each partition's tiles; tile_index[1, t] and tile_index[2, t] are row tiles below 8; tiles may repeat. `slot_counts`: some partition receives 8 live slots from every partition.
All inputs are finite; a program needn't handle non-finite values.
Results may differ from a plain program's by a relative error of at most 0.008.
Values may be sent and summed in bfloat16 or wider, within the bound.
A program may use at most 64 MiB of HBM per device.

v0:
```python
import jax
import jax.numpy as jnp
from jax import lax
from jax.sharding import PartitionSpec as P

TILE = 128
REACH = 4


def from_behind(block, axis, distance):
    devices = range(lax.axis_size(axis))
    route = [((i - distance) % len(devices), i) for i in devices]
    return lax.ppermute(block, axis, route)


def body(
    features, tile_values, tile_index, send_rows, slot_counts, far_weight, weight_one, weight_two
):
    blocks = lax.axis_size("blk")
    position = lax.axis_index("blk")
    own_width = features.shape[1]
    column_start = lax.axis_index("col") * own_width
    row_count = features.shape[0]
    row_tiles = row_count // TILE
    tile_count = tile_values.shape[0]
    per_block = tile_count // row_tiles
    capacity = send_rows.shape[2]
    stacked_tiles = (2 * REACH + 1) * row_tiles
    offset_slot = (tile_index[0] - position + REACH) % blocks
    source_row_tile = (offset_slot * row_tiles + tile_index[1]).reshape(row_tiles, per_block)
    target_blocks = tile_index[2].reshape(row_tiles, per_block)
    value_blocks = tile_values.reshape(row_tiles, per_block, TILE, TILE)
    live_slots = (jnp.arange(capacity, dtype=jnp.int32)[None, :] < slot_counts[0][:, None]).reshape(
        -1
    )
    list_rows = send_rows[0].reshape(-1)
    row_numbers = jnp.arange(row_count, dtype=jnp.int32)
    pick_rows = ((list_rows[:, None] == row_numbers[None, :]) & live_slots[:, None]).astype(
        jnp.bfloat16
    )
    stacked_numbers = jnp.arange(stacked_tiles, dtype=jnp.int32)
    target_numbers = jnp.arange(row_tiles, dtype=jnp.int32)

    def aggregate(field):
        outgoing = jnp.dot(pick_rows, field, preferred_element_type=jnp.float32).astype(
            jnp.bfloat16
        )
        outgoing = outgoing.reshape(blocks, capacity, own_width)
        arrived = lax.all_to_all(outgoing, "blk", split_axis=0, concat_axis=0, tiled=True)
        gathered = [
            from_behind(field, "blk", -offset) if offset != 0 else field
            for offset in range(-REACH, REACH + 1)
        ]
        stacked = jnp.stack(gathered).reshape(stacked_tiles, TILE, own_width)

        def add_block(total, packed):
            values_block, source_block, target_block = packed
            select_table = (source_block[:, None] == stacked_numbers[None, :]).astype(jnp.bfloat16)
            sources = jnp.einsum(
                "ts,sjc->tjc", select_table, stacked, preferred_element_type=jnp.float32
            ).astype(jnp.bfloat16)
            products = jnp.einsum(
                "tij,tjc->tic", values_block, sources, preferred_element_type=jnp.float32
            )
            place_table = (target_numbers[:, None] == target_block[None, :]).astype(jnp.float32)
            placed = jnp.einsum(
                "rt,tic->ric", place_table, products, precision=lax.Precision.HIGHEST
            )
            return (total + placed, None)

        empty = jnp.zeros((row_tiles, TILE, own_width), jnp.float32)
        near_term, unused = lax.scan(
            add_block, empty, (value_blocks, source_row_tile, target_blocks)
        )
        far_term = jnp.dot(
            far_weight,
            arrived.reshape(blocks * capacity, own_width),
            preferred_element_type=jnp.float32,
        )
        return (near_term.reshape(row_count, own_width) + far_term).astype(jnp.bfloat16)

    def project(aggregated, weights):
        piece = lax.all_gather(aggregated, "col", axis=1, tiled=True)
        rows_part = lax.dynamic_slice(weights, (0, column_start), (piece.shape[1], own_width))
        return jnp.dot(piece, rows_part, preferred_element_type=jnp.float32)

    first = aggregate(features)
    hidden = jnp.maximum(project(first, weight_one), 0.0).astype(jnp.bfloat16)
    second = aggregate(hidden)
    return project(second, weight_two).astype(jnp.bfloat16)


def solution(mesh):
    placed = (
        P("blk", "col"),
        P("blk", None, None),
        P(None, "blk"),
        P("blk", None, None),
        P("blk", None),
        P("blk", None),
        P(),
        P(),
    )
    return jax.shard_map(
        body, mesh=mesh, in_specs=placed, out_specs=P("blk", "col"), check_vma=False
    )
```

profile of v0, /device:TPU:1, one launch (start us, length us, event | category | flops | bytes accessed | tf_op | source)
XLA Modules:
  0.0 307.3 jit_solution(8751674541607003753)
XLA Ops:
  0.0 3.9 %collective-permute-start = (bf16[1024,128]{1,0:T(8,128)(2,1)}, bf16[1024,128]{1,0:T(8,128)(2,1)}, u32[]{:S(2)}, u32[]{:S(2)}) collective-permute-start(bf16[1024,128]{1,0:T(8,128)(2,1)} %param.12), channel_id=1, source_target_pairs={{248,0},{250,2},{252,4},{254,6},{0,8},{2,10},{4,12},{6,14},{8,16},... | collective-permute-start | bytes 786440 | tf_op jit(solution)/shard_map/ppermute | solution.py:13
  3.9 5.0 %collective-permute-start.1 = (bf16[1024,128]{1,0:T(8,128)(2,1)}, bf16[1024,128]{1,0:T(8,128)(2,1)}, u32[]{:S(2)}, u32[]{:S(2)}) collective-permute-start(bf16[1024,128]{1,0:T(8,128)(2,1)} %param.12), channel_id=1, source_target_pairs={{250,0},{252,2},{254,4},{0,6},{2,8},{4,10},{6,12},{8,14},{10,16},{... | collective-permute-start | bytes 786440 | tf_op jit(solution)/shard_map/ppermute | solution.py:13
  14.9 12.5 %all-to-all-start = ((bf16[128,8,128]{2,1,0:T(8,128)(2,1)}), bf16[128,8,128]{2,1,0:T(8,128)(2,1)S(1)}, u32[]{:S(2)}, u32[]{:S(2)}) async-start(bf16[128,8,128]{2,1,0:T(8,128)(2,1)} %fusion.69), calls=%async_computation | async-start | bytes 524288 | tf_op jit(solution)/shard_map/all_to_all | solution.py:49
  27.7 7.9 %collective-permute-start.5 = (bf16[1024,128]{1,0:T(8,128)(2,1)S(1)}, bf16[1024,128]{1,0:T(8,128)(2,1)S(1)}, u32[]{:S(2)}, u32[]{:S(2)}) collective-permute-start(bf16[1024,128]{1,0:T(8,128)(2,1)S(1)} %copy-done.3), channel_id=1, source_target_pairs={{4,0},{6,2},{8,4},{10,6},{12,8},{14,10},{16,12},{18,14},{20,16},{2... | collective-permute-start | bytes 786440 | tf_op jit(solution)/shard_map/ppermute | solution.py:13
  43.9 11.9 %collective-permute-done.6 = bf16[1024,128]{1,0:T(8,128)(2,1)S(1)} collective-permute-done((bf16[1024,128]{1,0:T(8,128)(2,1)S(1)}, bf16[1024,128]{1,0:T(8,128)(2,1)S(1)}, u32[]{:S(2)}, u32[]{:S(2)}) %collective-permute-start.6) | collective-permute-done | bytes 262176 | tf_op jit(solution)/shard_map/ppermute | solution.py:13
  55.8 5.3 %collective-permute-done.7 = bf16[1024,128]{1,0:T(8,128)(2,1)S(1)} collective-permute-done((bf16[1024,128]{1,0:T(8,128)(2,1)S(1)}, bf16[1024,128]{1,0:T(8,128)(2,1)S(1)}, u32[]{:S(2)}, u32[]{:S(2)}) %collective-permute-start.7) | collective-permute-done | bytes 262176 | tf_op jit(solution)/shard_map/ppermute | solution.py:13
  62.6 85.1 %while.22 = (s32[]{:T(128)}, f32[8,128,128]{2,0,1:T(8,128)S(1)}, s32[8,36]{1,0:T(8,128)S(1)}, bf16[8,36,128,128]{3,2,1,0:T(8,128)(2,1)}, s32[8,36]{1,0:T(8,128)S...) while((s32[]{:T(128)}, f32[8,128,128]{2,0,1:T(8,128)S(1)}, s32[8,36]{1,0:T(8,128)S(1)}, ...), condition=%wide.region_1.2_spmd.clone, body=%wide.region_0.1_spmd.clone.sunk | while | flops 292817728 | bytes 11666883 | solution.py:72
  69.3 3.9 %fusion.113 = f32[8,128,128]{2,0,1:T(8,128)S(1)} fusion(f32[36,128,128]{2,1,0:T(8,128)} %fusion.112, f32[8,128,128]{2,0,1:T(8,128)S(1)} %get-tuple-element.263, pred[]{:T(512)S(6)} %compare.7, s32[36]{0:T(128)S(1)} %get-tuple-element.245), kind=kOutput, calls=%fused_computation.9.clone.1 | convolution fusion | flops 56885536 | bytes 3408017 | tf_op jit(solution)/shard_map/while/body/eval_jaxpr/rt,tic->ric/dot_general | solution.py:66
  80.0 3.9 %fusion.113 = f32[8,128,128]{2,0,1:T(8,128)S(1)} fusion(f32[36,128,128]{2,1,0:T(8,128)} %fusion.112, f32[8,128,128]{2,0,1:T(8,128)S(1)} %get-tuple-element.263, pred[]{:T(512)S(6)} %compare.7, s32[36]{0:T(128)S(1)} %get-tuple-element.245), kind=kOutput, calls=%fused_computation.9.clone.1 | convolution fusion | flops 56885536 | bytes 3408017 | tf_op jit(solution)/shard_map/while/body/eval_jaxpr/rt,tic->ric/dot_general | solution.py:66
  90.6 3.9 %fusion.113 = f32[8,128,128]{2,0,1:T(8,128)S(1)} fusion(f32[36,128,128]{2,1,0:T(8,128)} %fusion.112, f32[8,128,128]{2,0,1:T(8,128)S(1)} %get-tuple-element.263, pred[]{:T(512)S(6)} %compare.7, s32[36]{0:T(128)S(1)} %get-tuple-element.245), kind=kOutput, calls=%fused_computation.9.clone.1 | convolution fusion | flops 56885536 | bytes 3408017 | tf_op jit(solution)/shard_map/while/body/eval_jaxpr/rt,tic->ric/dot_general | solution.py:66
  101.2 3.9 %fusion.113 = f32[8,128,128]{2,0,1:T(8,128)S(1)} fusion(f32[36,128,128]{2,1,0:T(8,128)} %fusion.112, f32[8,128,128]{2,0,1:T(8,128)S(1)} %get-tuple-element.263, pred[]{:T(512)S(6)} %compare.7, s32[36]{0:T(128)S(1)} %get-tuple-element.245), kind=kOutput, calls=%fused_computation.9.clone.1 | convolution fusion | flops 56885536 | bytes 3408017 | tf_op jit(solution)/shard_map/while/body/eval_jaxpr/rt,tic->ric/dot_general | solution.py:66
  105.2 3.5 %fusion.111 = bf16[36,128,128]{2,0,1:T(8,128)(2,1)S(1)} fusion(bf16[72,128,128]{2,1,0:T(8,128)(2,1)} %get-tuple-element.275, s32[36]{0:T(128)S(1)} %get-tuple-element.244), kind=kOutput, calls=%fused_computation.7.clone.1 | convolution fusion | flops 84937248 | bytes 3539088 | tf_op jit(solution)/shard_map/while/body/eval_jaxpr/ts,sjc->tjc/dot_general | solution.py:59
  111.9 3.9 %fusion.113 = f32[8,128,128]{2,0,1:T(8,128)S(1)} fusion(f32[36,128,128]{2,1,0:T(8,128)} %fusion.112, f32[8,128,128]{2,0,1:T(8,128)S(1)} %get-tuple-element.263, pred[]{:T(512)S(6)} %compare.7, s32[36]{0:T(128)S(1)} %get-tuple-element.245), kind=kOutput, calls=%fused_computation.9.clone.1 | convolution fusion | flops 56885536 | bytes 3408017 | tf_op jit(solution)/shard_map/while/body/eval_jaxpr/rt,tic->ric/dot_general | solution.py:66
  122.5 3.9 %fusion.113 = f32[8,128,128]{2,0,1:T(8,128)S(1)} fusion(f32[36,128,128]{2,1,0:T(8,128)} %fusion.112, f32[8,128,128]{2,0,1:T(8,128)S(1)} %get-tuple-element.263, pred[]{:T(512)S(6)} %compare.7, s32[36]{0:T(128)S(1)} %get-tuple-element.245), kind=kOutput, calls=%fused_computation.9.clone.1 | convolution fusion | flops 56885536 | bytes 3408017 | tf_op jit(solution)/shard_map/while/body/eval_jaxpr/rt,tic->ric/dot_general | solution.py:66
  133.2 3.9 %fusion.113 = f32[8,128,128]{2,0,1:T(8,128)S(1)} fusion(f32[36,128,128]{2,1,0:T(8,128)} %fusion.112, f32[8,128,128]{2,0,1:T(8,128)S(1)} %get-tuple-element.263, pred[]{:T(512)S(6)} %compare.7, s32[36]{0:T(128)S(1)} %get-tuple-element.245), kind=kOutput, calls=%fused_computation.9.clone.1 | convolution fusion | flops 56885536 | bytes 3408017 | tf_op jit(solution)/shard_map/while/body/eval_jaxpr/rt,tic->ric/dot_general | solution.py:66
  143.8 3.9 %fusion.113 = f32[8,128,128]{2,0,1:T(8,128)S(1)} fusion(f32[36,128,128]{2,1,0:T(8,128)} %fusion.112, f32[8,128,128]{2,0,1:T(8,128)S(1)} %get-tuple-element.263, pred[]{:T(512)S(6)} %compare.7, s32[36]{0:T(128)S(1)} %get-tuple-element.245), kind=kOutput, calls=%fused_computation.9.clone.1 | convolution fusion | flops 56885536 | bytes 3408017 | tf_op jit(solution)/shard_map/while/body/eval_jaxpr/rt,tic->ric/dot_general | solution.py:66
  148.6 7.4 %all_gather.6 = bf16[1024,256]{1,0:T(8,128)(2,1)S(1)} all-gather(bf16[1024,128]{1,0:T(8,128)(2,1)S(1)} %fusion.65), channel_id=1, replica_groups=mesh['blk'=128,'col'=2] {'col'}, dimensions={1}, use_global_device_ids=true | all-gather | bytes 786432 | tf_op jit(solution)/shard_map/all_gather | solution.py:83
  156.2 3.9 %collective-permute-start.8 = (bf16[1024,128]{1,0:T(8,128)(2,1)S(1)}, bf16[1024,128]{1,0:T(8,128)(2,1)}, u32[]{:S(2)}, u32[]{:S(2)}) collective-permute-start(bf16[1024,128]{1,0:T(8,128)(2,1)S(1)} %fusion.63), channel_id=1, source_target_pairs={{248,0},{250,2},{252,4},{254,6},{0,8},{2,10},{4,12},{6,14},{8,16},... | collective-permute-start | bytes 786440 | tf_op jit(solution)/shard_map/ppermute | solution.py:13
  164.4 13.6 %all-to-all-start.1 = ((bf16[128,8,128]{2,1,0:T(8,128)(2,1)}), bf16[128,8,128]{2,1,0:T(8,128)(2,1)S(1)}, u32[]{:S(2)}, u32[]{:S(2)}) async-start(bf16[128,8,128]{2,1,0:T(8,128)(2,1)} %fusion.66), calls=%async_computation.1 | async-start | bytes 524288 | tf_op jit(solution)/shard_map/all_to_all | solution.py:49
  178.0 7.9 %collective-permute-start.13 = (bf16[1024,128]{1,0:T(8,128)(2,1)S(1)}, bf16[1024,128]{1,0:T(8,128)(2,1)S(1)}, u32[]{:S(2)}, u32[]{:S(2)}) collective-permute-start(bf16[1024,128]{1,0:T(8,128)(2,1)S(1)} %fusion.63), channel_id=1, source_target_pairs={{4,0},{6,2},{8,4},{10,6},{12,8},{14,10},{16,12},{18,14},{20,16},{2... | collective-permute-start | bytes 786440 | tf_op jit(solution)/shard_map/ppermute | solution.py:13
  193.9 12.4 %collective-permute-done.14 = bf16[1024,128]{1,0:T(8,128)(2,1)S(1)} collective-permute-done((bf16[1024,128]{1,0:T(8,128)(2,1)S(1)}, bf16[1024,128]{1,0:T(8,128)(2,1)S(1)}, u32[]{:S(2)}, u32[]{:S(2)}) %collective-permute-start.14) | collective-permute-done | bytes 262176 | tf_op jit(solution)/shard_map/ppermute | solution.py:13
  206.3 5.1 %collective-permute-done.15 = bf16[1024,128]{1,0:T(8,128)(2,1)S(1)} collective-permute-done((bf16[1024,128]{1,0:T(8,128)(2,1)S(1)}, bf16[1024,128]{1,0:T(8,128)(2,1)S(1)}, u32[]{:S(2)}, u32[]{:S(2)}) %collective-permute-start.15) | collective-permute-done | bytes 262176 | tf_op jit(solution)/shard_map/ppermute | solution.py:13
  213.0 85.1 %while.23 = (s32[]{:T(128)}, f32[8,128,128]{2,0,1:T(8,128)S(1)}, s32[8,36]{1,0:T(8,128)S(1)}, bf16[8,36,128,128]{3,2,1,0:T(8,128)(2,1)}, s32[8,36]{1,0:T(8,128)S...) while((s32[]{:T(128)}, f32[8,128,128]{2,0,1:T(8,128)S(1)}, s32[8,36]{1,0:T(8,128)S(1)}, ...), condition=%wide.region_3.4_spmd.clone, body=%wide.region_2.3_spmd.clone.sunk | while | flops 292817728 | bytes 11666883 | solution.py:72
  219.7 3.9 %fusion.122 = f32[8,128,128]{2,0,1:T(8,128)S(1)} fusion(f32[36,128,128]{2,1,0:T(8,128)} %fusion.121, f32[8,128,128]{2,0,1:T(8,128)S(1)} %get-tuple-element.287, pred[]{:T(512)S(6)} %compare.8, s32[36]{0:T(128)S(1)} %get-tuple-element.253), kind=kOutput, calls=%fused_computation.29.clone.1 | convolution fusion | flops 56885536 | bytes 3408017 | tf_op jit(solution)/shard_map/while/body/eval_jaxpr/rt,tic->ric/dot_general | solution.py:66
  230.3 3.9 %fusion.122 = f32[8,128,128]{2,0,1:T(8,128)S(1)} fusion(f32[36,128,128]{2,1,0:T(8,128)} %fusion.121, f32[8,128,128]{2,0,1:T(8,128)S(1)} %get-tuple-element.287, pred[]{:T(512)S(6)} %compare.8, s32[36]{0:T(128)S(1)} %get-tuple-element.253), kind=kOutput, calls=%fused_computation.29.clone.1 | convolution fusion | flops 56885536 | bytes 3408017 | tf_op jit(solution)/shard_map/while/body/eval_jaxpr/rt,tic->ric/dot_general | solution.py:66
  240.9 3.9 %fusion.122 = f32[8,128,128]{2,0,1:T(8,128)S(1)} fusion(f32[36,128,128]{2,1,0:T(8,128)} %fusion.121, f32[8,128,128]{2,0,1:T(8,128)S(1)} %get-tuple-element.287, pred[]{:T(512)S(6)} %compare.8, s32[36]{0:T(128)S(1)} %get-tuple-element.253), kind=kOutput, calls=%fused_computation.29.clone.1 | convolution fusion | flops 56885536 | bytes 3408017 | tf_op jit(solution)/shard_map/while/body/eval_jaxpr/rt,tic->ric/dot_general | solution.py:66
  251.6 3.9 %fusion.122 = f32[8,128,128]{2,0,1:T(8,128)S(1)} fusion(f32[36,128,128]{2,1,0:T(8,128)} %fusion.121, f32[8,128,128]{2,0,1:T(8,128)S(1)} %get-tuple-element.287, pred[]{:T(512)S(6)} %compare.8, s32[36]{0:T(128)S(1)} %get-tuple-element.253), kind=kOutput, calls=%fused_computation.29.clone.1 | convolution fusion | flops 56885536 | bytes 3408017 | tf_op jit(solution)/shard_map/while/body/eval_jaxpr/rt,tic->ric/dot_general | solution.py:66
  262.2 3.9 %fusion.122 = f32[8,128,128]{2,0,1:T(8,128)S(1)} fusion(f32[36,128,128]{2,1,0:T(8,128)} %fusion.121, f32[8,128,128]{2,0,1:T(8,128)S(1)} %get-tuple-element.287, pred[]{:T(512)S(6)} %compare.8, s32[36]{0:T(128)S(1)} %get-tuple-element.253), kind=kOutput, calls=%fused_computation.29.clone.1 | convolution fusion | flops 56885536 | bytes 3408017 | tf_op jit(solution)/shard_map/while/body/eval_jaxpr/rt,tic->ric/dot_general | solution.py:66
  272.9 3.9 %fusion.122 = f32[8,128,128]{2,0,1:T(8,128)S(1)} fusion(f32[36,128,128]{2,1,0:T(8,128)} %fusion.121, f32[8,128,128]{2,0,1:T(8,128)S(1)} %get-tuple-element.287, pred[]{:T(512)S(6)} %compare.8, s32[36]{0:T(128)S(1)} %get-tuple-element.253), kind=kOutput, calls=%fused_computation.29.clone.1 | convolution fusion | flops 56885536 | bytes 3408017 | tf_op jit(solution)/shard_map/while/body/eval_jaxpr/rt,tic->ric/dot_general | solution.py:66
  283.5 3.9 %fusion.122 = f32[8,128,128]{2,0,1:T(8,128)S(1)} fusion(f32[36,128,128]{2,1,0:T(8,128)} %fusion.121, f32[8,128,128]{2,0,1:T(8,128)S(1)} %get-tuple-element.287, pred[]{:T(512)S(6)} %compare.8, s32[36]{0:T(128)S(1)} %get-tuple-element.253), kind=kOutput, calls=%fused_computation.29.clone.1 | convolution fusion | flops 56885536 | bytes 3408017 | tf_op jit(solution)/shard_map/while/body/eval_jaxpr/rt,tic->ric/dot_general | solution.py:66
  294.1 3.9 %fusion.122 = f32[8,128,128]{2,0,1:T(8,128)S(1)} fusion(f32[36,128,128]{2,1,0:T(8,128)} %fusion.121, f32[8,128,128]{2,0,1:T(8,128)S(1)} %get-tuple-element.287, pred[]{:T(512)S(6)} %compare.8, s32[36]{0:T(128)S(1)} %get-tuple-element.253), kind=kOutput, calls=%fused_computation.29.clone.1 | convolution fusion | flops 56885536 | bytes 3408017 | tf_op jit(solution)/shard_map/while/body/eval_jaxpr/rt,tic->ric/dot_general | solution.py:66
  298.9 7.4 %all_gather.7 = bf16[1024,256]{1,0:T(8,128)(2,1)S(1)} all-gather(bf16[1024,128]{1,0:T(8,128)(2,1)S(1)} %fusion.64), channel_id=1, replica_groups=mesh['blk'=128,'col'=2] {'col'}, dimensions={1}, use_global_device_ids=true | all-gather | bytes 786432 | tf_op jit(solution)/shard_map/all_gather | solution.py:83
  (123 shorter events, 136.4 us)
Async XLA Ops:
  0.0 147.8 %copy-start = (bf16[1024,1024]{1,0:T(8,128)(2,1)S(1)}, bf16[1024,1024]{1,0:T(8,128)(2,1)}, u32[]{:S(2)}) copy-start(bf16[1024,1024]{1,0:T(8,128)(2,1)} %param.17) | copy-start | bytes 6291460
  0.0 27.7 %copy-start.3 = (bf16[1024,128]{1,0:T(8,128)(2,1)S(1)}, bf16[1024,128]{1,0:T(8,128)(2,1)}, u32[]{:S(2)}) copy-start(bf16[1024,128]{1,0:T(8,128)(2,1)} %param.12) | copy-start | bytes 786436
  0.0 27.4 %copy-start.6 = (s32[3,288]{1,0:T(4,128)S(1)}, s32[3,288]{1,0:T(4,128)}, u32[]{:S(2)}) copy-start(s32[3,288]{1,0:T(4,128)} %param.14) | copy-start | bytes 10372
  0.0 27.7 %collective-permute-start = (bf16[1024,128]{1,0:T(8,128)(2,1)}, bf16[1024,128]{1,0:T(8,128)(2,1)}, u32[]{:S(2)}, u32[]{:S(2)}) collective-permute-start(bf16[1024,128]{1,0:T(8,128)(2,1)} %param.12), channel_id=1, source_target_pairs={{248,0},{250,2},{252,4},{254,6},{0,8},{2,10},{4,12},{6,14},{8,16},... | collective-permute-start | bytes 786440 | tf_op jit(solution)/shard_map/ppermute | solution.py:13
  3.9 32.7 %collective-permute-start.1 = (bf16[1024,128]{1,0:T(8,128)(2,1)}, bf16[1024,128]{1,0:T(8,128)(2,1)}, u32[]{:S(2)}, u32[]{:S(2)}) collective-permute-start(bf16[1024,128]{1,0:T(8,128)(2,1)} %param.12), channel_id=1, source_target_pairs={{250,0},{252,2},{254,4},{0,6},{2,8},{4,10},{6,12},{8,14},{10,16},{... | collective-permute-start | bytes 786440 | tf_op jit(solution)/shard_map/ppermute | solution.py:13
  9.0 30.5 %collective-permute-start.2 = (bf16[1024,128]{1,0:T(8,128)(2,1)}, bf16[1024,128]{1,0:T(8,128)(2,1)}, u32[]{:S(2)}, u32[]{:S(2)}) collective-permute-start(bf16[1024,128]{1,0:T(8,128)(2,1)} %param.12), channel_id=1, source_target_pairs={{252,0},{254,2},{0,4},{2,6},{4,8},{6,10},{8,12},{10,14},{12,16},{1... | collective-permute-start | bytes 786440 | tf_op jit(solution)/shard_map/ppermute | solution.py:13
  9.7 33.0 %collective-permute-start.3 = (bf16[1024,128]{1,0:T(8,128)(2,1)}, bf16[1024,128]{1,0:T(8,128)(2,1)}, u32[]{:S(2)}, u32[]{:S(2)}) collective-permute-start(bf16[1024,128]{1,0:T(8,128)(2,1)} %param.12), channel_id=1, source_target_pairs={{254,0},{0,2},{2,4},{4,6},{6,8},{8,10},{10,12},{12,14},{14,16},{16... | collective-permute-start | bytes 786440 | tf_op jit(solution)/shard_map/ppermute | solution.py:13
  9.7 34.0 %collective-permute-start.4 = (bf16[1024,128]{1,0:T(8,128)(2,1)}, bf16[1024,128]{1,0:T(8,128)(2,1)S(1)}, u32[]{:S(2)}, u32[]{:S(2)}) collective-permute-start(bf16[1024,128]{1,0:T(8,128)(2,1)} %param.12), channel_id=1, source_target_pairs={{2,0},{4,2},{6,4},{8,6},{10,8},{12,10},{14,12},{16,14},{18,16},{20... | collective-permute-start | bytes 786440 | tf_op jit(solution)/shard_map/ppermute | solution.py:13
  14.9 132.9 %all-to-all-start = ((bf16[128,8,128]{2,1,0:T(8,128)(2,1)}), bf16[128,8,128]{2,1,0:T(8,128)(2,1)S(1)}, u32[]{:S(2)}, u32[]{:S(2)}) async-start(bf16[128,8,128]{2,1,0:T(8,128)(2,1)} %fusion.69), calls=%async_computation | async-start | bytes 524288 | tf_op jit(solution)/shard_map/all_to_all | solution.py:49
  27.7 16.1 %collective-permute-start.5 = (bf16[1024,128]{1,0:T(8,128)(2,1)S(1)}, bf16[1024,128]{1,0:T(8,128)(2,1)S(1)}, u32[]{:S(2)}, u32[]{:S(2)}) collective-permute-start(bf16[1024,128]{1,0:T(8,128)(2,1)S(1)} %copy-done.3), channel_id=1, source_target_pairs={{4,0},{6,2},{8,4},{10,6},{12,8},{14,10},{16,12},{18,14},{20,16},{2... | collective-permute-start | bytes 786440 | tf_op jit(solution)/shard_map/ppermute | solution.py:13
  36.6 19.1 %collective-permute-start.6 = (bf16[1024,128]{1,0:T(8,128)(2,1)S(1)}, bf16[1024,128]{1,0:T(8,128)(2,1)S(1)}, u32[]{:S(2)}, u32[]{:S(2)}) collective-permute-start(bf16[1024,128]{1,0:T(8,128)(2,1)S(1)} %copy-done.3), channel_id=1, source_target_pairs={{6,0},{8,2},{10,4},{12,6},{14,8},{16,10},{18,12},{20,14},{22,16},{... | collective-permute-start | bytes 786440 | tf_op jit(solution)/shard_map/ppermute | solution.py:13
  39.4 21.7 %collective-permute-start.7 = (bf16[1024,128]{1,0:T(8,128)(2,1)S(1)}, bf16[1024,128]{1,0:T(8,128)(2,1)S(1)}, u32[]{:S(2)}, u32[]{:S(2)}) collective-permute-start(bf16[1024,128]{1,0:T(8,128)(2,1)S(1)} %copy-done.3), channel_id=1, source_target_pairs={{8,0},{10,2},{12,4},{14,6},{16,8},{18,10},{20,12},{22,14},{24,16},... | collective-permute-start | bytes 786440 | tf_op jit(solution)/shard_map/ppermute | solution.py:13
  61.2 1.4 copy-start.1
  147.7 8.2 %copy-start.4 = (bf16[256,256]{1,0:T(8,128)(2,1)S(1)}, bf16[256,256]{1,0:T(8,128)(2,1)}, u32[]{:S(2)}) copy-start(bf16[256,256]{1,0:T(8,128)(2,1)} %param.18) | copy-start | bytes 393220
  156.2 21.8 %collective-permute-start.8 = (bf16[1024,128]{1,0:T(8,128)(2,1)S(1)}, bf16[1024,128]{1,0:T(8,128)(2,1)}, u32[]{:S(2)}, u32[]{:S(2)}) collective-permute-start(bf16[1024,128]{1,0:T(8,128)(2,1)S(1)} %fusion.63), channel_id=1, source_target_pairs={{248,0},{250,2},{252,4},{254,6},{0,8},{2,10},{4,12},{6,14},{8,16},... | collective-permute-start | bytes 786440 | tf_op jit(solution)/shard_map/ppermute | solution.py:13
  160.1 26.8 %collective-permute-start.9 = (bf16[1024,128]{1,0:T(8,128)(2,1)S(1)}, bf16[1024,128]{1,0:T(8,128)(2,1)}, u32[]{:S(2)}, u32[]{:S(2)}) collective-permute-start(bf16[1024,128]{1,0:T(8,128)(2,1)S(1)} %fusion.63), channel_id=1, source_target_pairs={{250,0},{252,2},{254,4},{0,6},{2,8},{4,10},{6,12},{8,14},{10,16},{... | collective-permute-start | bytes 786440 | tf_op jit(solution)/shard_map/ppermute | solution.py:13
  161.9 27.8 %collective-permute-start.10 = (bf16[1024,128]{1,0:T(8,128)(2,1)S(1)}, bf16[1024,128]{1,0:T(8,128)(2,1)}, u32[]{:S(2)}, u32[]{:S(2)}) collective-permute-start(bf16[1024,128]{1,0:T(8,128)(2,1)S(1)} %fusion.63), channel_id=1, source_target_pairs={{252,0},{254,2},{0,4},{2,6},{4,8},{6,10},{8,12},{10,14},{12,16},{1... | collective-permute-start | bytes 786440 | tf_op jit(solution)/shard_map/ppermute | solution.py:13
  161.9 30.9 %collective-permute-start.11 = (bf16[1024,128]{1,0:T(8,128)(2,1)S(1)}, bf16[1024,128]{1,0:T(8,128)(2,1)}, u32[]{:S(2)}, u32[]{:S(2)}) collective-permute-start(bf16[1024,128]{1,0:T(8,128)(2,1)S(1)} %fusion.63), channel_id=1, source_target_pairs={{254,0},{0,2},{2,4},{4,6},{6,8},{8,10},{10,12},{12,14},{14,16},{16... | collective-permute-start | bytes 786440 | tf_op jit(solution)/shard_map/ppermute | solution.py:13
  162.4 31.4 %collective-permute-start.12 = (bf16[1024,128]{1,0:T(8,128)(2,1)S(1)}, bf16[1024,128]{1,0:T(8,128)(2,1)S(1)}, u32[]{:S(2)}, u32[]{:S(2)}) collective-permute-start(bf16[1024,128]{1,0:T(8,128)(2,1)S(1)} %fusion.63), channel_id=1, source_target_pairs={{2,0},{4,2},{6,4},{8,6},{10,8},{12,10},{14,12},{16,14},{18,16},{20... | collective-permute-start | bytes 786440 | tf_op jit(solution)/shard_map/ppermute | solution.py:13
  164.4 133.8 %all-to-all-start.1 = ((bf16[128,8,128]{2,1,0:T(8,128)(2,1)}), bf16[128,8,128]{2,1,0:T(8,128)(2,1)S(1)}, u32[]{:S(2)}, u32[]{:S(2)}) async-start(bf16[128,8,128]{2,1,0:T(8,128)(2,1)} %fusion.66), calls=%async_computation.1 | async-start | bytes 524288 | tf_op jit(solution)/shard_map/all_to_all | solution.py:49
  178.0 15.9 %collective-permute-start.13 = (bf16[1024,128]{1,0:T(8,128)(2,1)S(1)}, bf16[1024,128]{1,0:T(8,128)(2,1)S(1)}, u32[]{:S(2)}, u32[]{:S(2)}) collective-permute-start(bf16[1024,128]{1,0:T(8,128)(2,1)S(1)} %fusion.63), channel_id=1, source_target_pairs={{4,0},{6,2},{8,4},{10,6},{12,8},{14,10},{16,12},{18,14},{20,16},{2... | collective-permute-start | bytes 786440 | tf_op jit(solution)/shard_map/ppermute | solution.py:13
  186.9 19.4 %collective-permute-start.14 = (bf16[1024,128]{1,0:T(8,128)(2,1)S(1)}, bf16[1024,128]{1,0:T(8,128)(2,1)S(1)}, u32[]{:S(2)}, u32[]{:S(2)}) collective-permute-start(bf16[1024,128]{1,0:T(8,128)(2,1)S(1)} %fusion.63), channel_id=1, source_target_pairs={{6,0},{8,2},{10,4},{12,6},{14,8},{16,10},{18,12},{20,14},{22,16},{... | collective-permute-start | bytes 786440 | tf_op jit(solution)/shard_map/ppermute | solution.py:13
  189.7 21.8 %collective-permute-start.15 = (bf16[1024,128]{1,0:T(8,128)(2,1)S(1)}, bf16[1024,128]{1,0:T(8,128)(2,1)S(1)}, u32[]{:S(2)}, u32[]{:S(2)}) collective-permute-start(bf16[1024,128]{1,0:T(8,128)(2,1)S(1)} %fusion.63), channel_id=1, source_target_pairs={{8,0},{10,2},{12,4},{14,6},{16,8},{18,10},{20,12},{22,14},{24,16},... | collective-permute-start | bytes 786440 | tf_op jit(solution)/shard_map/ppermute | solution.py:13
  211.5 1.4 copy-start.2
  298.0 8.2 %copy-start.5 = (bf16[256,256]{1,0:T(8,128)(2,1)S(1)}, bf16[256,256]{1,0:T(8,128)(2,1)}, u32[]{:S(2)}) copy-start(bf16[256,256]{1,0:T(8,128)(2,1)} %param.19) | copy-start | bytes 393220
where the time goes:
time: 311 us; the launch traced here: 307 us
  matrix products  177 us (57%)
  starting transfers between devices  66.3 us (21%)
  waiting for transfers between devices  34.7 us (11%)
  blocking collectives  14.7 us (5%)
  local copies, waits for them, and re-layouts  12.6 us (4%)
    dot_general x16, matrix products, add_block(): jnp.einsum('rt,tic->ric', place_table, products, precision=lax.Precision....  62.3 us
    dot_general x16, matrix products, add_block(): jnp.einsum('ts,sjc->tjc', select_table, stacked, preferred_element_type=j...  56.4 us
    dot_general x16, matrix products, add_block(): jnp.einsum('tij,tjc->tic', values_block, sources, preferred_element_type=...  50.8 us
    ppermute x16, starting transfers between devices, from_behind(): return lax.ppermute(block, axis, route)  40.2 us
    ppermute x16, waiting for transfers between devices, from_behind(): return lax.ppermute(block, axis, route)  34.7 us
    all_to_all x2, starting transfers between devices, aggregate(): lax.all_to_all(outgoing, 'blk', split_axis=0, concat_axis=0, tiled=True)  26.1 us
    all_gather x2, blocking collectives, project(): piece = lax.all_gather(aggregated, 'col', axis=1, tiled=True)  14.7 us
    unnamed x31, local copies, waits for them, and re-layouts  11.8 us
  transfers between devices with their start and end apart: 18, of which 4 were waited for; matrix products, arithmetic and copies ran while one was open for 60% of the time, Pallas kernels for 0%

commit v1 on v0

v1 whole, which is shorter than its diff:
```python
import functools

import jax
import jax.numpy as jnp
from jax import lax
from jax.experimental import pallas as pl
from jax.experimental.pallas import tpu as pltpu
from jax.sharding import PartitionSpec as P

MESH = pl.DeviceIdType.MESH
BF16 = jnp.bfloat16
F32 = jnp.float32
TILE = 128
REACH = 4
SLOTS_NEAR = 2 * REACH + 1
ROW_TILES = 8
ROWS = 1024
WIDTH = 128
CHUNKS = 4
CHUNK = ROWS // CHUNKS
RING = 16
GROUPS = 8
EMPTY = 288


def dot(a, b):
    return jnp.dot(a, b, preferred_element_type=F32)


def kernel(
    blocks, table_ref, earlier_ref, lists_ref, x_hbm, tiles_hbm, far_hbm, w1_hbm, w2_hbm, out_ref,
    tiles, sums, far, w1, w2, field, total, pair, picks, outgoing, middle, sorted_out, landed, arrived,
    load_sem, near_send, near_recv, group_send, group_recv, ring_send, ring_recv, col_send, col_recv,
):
    blk = lax.axis_index("blk")
    col = lax.axis_index("col")
    core = lax.rem(blk, 2)
    up = lax.rem(blk + 2, blocks)
    down = lax.rem(blk + blocks - 2, blocks)
    sibling = blk + 1 - 2 * core
    place = lax.rem(blk, RING)
    ring_base = blk - place
    group = blk // RING

    x_load = pltpu.make_async_copy(x_hbm, field.at[0, 4], load_sem.at[0])
    tiles_load = pltpu.make_async_copy(tiles_hbm, tiles.at[pl.ds(0, EMPTY)], load_sem.at[1])
    w1_load = pltpu.make_async_copy(w1_hbm, w1, load_sem.at[2])
    w2_load = pltpu.make_async_copy(w2_hbm, w2, load_sem.at[3])
    far_load = pltpu.make_async_copy(far_hbm, far, load_sem.at[4])
    x_load.start()
    tiles_load.start()
    far_load.start()
    w1_load.start()
    w2_load.start()

    barrier = pltpu.get_barrier_semaphore()

    def greet(**device):
        pl.semaphore_signal(barrier, inc=1, device_id=device, device_id_type=MESH)

    for k in range(1, RING):
        greet(blk=ring_base + lax.rem(place + k, RING))
    for k in range(1, GROUPS):
        greet(blk=lax.rem(group + k, GROUPS) * RING + place)
    greet(blk=up)
    greet(blk=down)
    greet(col=1 - col)

    def remote(src, dst, send, recv, **device):
        return pltpu.make_async_remote_copy(
            src_ref=src, dst_ref=dst, send_sem=send, recv_sem=recv, device_id=device, device_id_type=MESH
        )

    for a in range(ROW_TILES):
        column = jnp.broadcast_to(lists_ref[a : a + 1, :], (TILE, TILE)).T
        for b in range(ROW_TILES):
            numbers = lax.broadcasted_iota(jnp.int32, (TILE, TILE), 1) + b * TILE
            picks[a * TILE : (a + 1) * TILE, b * TILE : (b + 1) * TILE] = jnp.where(
                column == numbers, 1.0, 0.0
            ).astype(BF16)

    def pick(layer):
        for a in range(CHUNKS):
            rows = dot(picks[a * CHUNK : (a + 1) * CHUNK, :], field[layer, 4])
            outgoing[layer, 2 * a : 2 * a + 2] = rows.astype(BF16).reshape(2, TILE, WIDTH)
        middle[layer, group] = outgoing[layer, group]

    def send_groups(layer):
        for k in range(1, GROUPS):
            other = lax.rem(group + k, GROUPS)
            remote(
                outgoing.at[layer, other], middle.at[layer, group],
                group_send.at[layer], group_recv.at[layer], blk=other * RING + place,
            ).start()

    def send_ring(layer):
        part = pl.ds(0, GROUPS - 1)
        remote(
            outgoing.at[layer, part], middle.at[layer, part], group_send.at[layer], group_recv.at[layer], blk=sibling
        ).wait_recv()
        rows = middle[layer].astype(F32).reshape(GROUPS, RING, 8, WIDTH)
        sorted_out[layer] = rows.transpose(1, 0, 2, 3).reshape(RING, GROUPS * 8, WIDTH).astype(BF16)
        landed[layer, place] = sorted_out[layer, place]
        for k in range(1, RING):
            other = lax.rem(place + k, RING)
            remote(
                sorted_out.at[layer, other], landed.at[layer, place],
                ring_send.at[layer], ring_recv.at[layer], blk=ring_base + other,
            ).start()

    def collect(layer):
        part = pl.ds(0, RING - 1)
        remote(
            sorted_out.at[layer, part], landed.at[layer, part], ring_send.at[layer], ring_recv.at[layer], blk=sibling
        ).wait_recv()
        rows = landed[layer].astype(F32).reshape(RING, GROUPS, 8, WIDTH)
        arrived[...] = rows.transpose(1, 0, 2, 3).reshape(ROWS, WIDTH).astype(BF16)

    def chunk(j):
        return pl.ds(pl.multiple_of(j * CHUNK, CHUNK), CHUNK)

    def send_near(layer, kind, j, source, target, device):
        remote(
            field.at[layer, source, chunk(j)], field.at[layer, target, chunk(j)],
            near_send.at[layer, kind], near_recv.at[layer, target, j], blk=device,
        ).start()

    def send_own(layer, j):
        send_near(layer, 0, j, 4, 2, up)
        send_near(layer, 1, j, 4, 6, down)
        send_near(layer, 2, j, 4, 3 + 2 * core, sibling)

    def wait_near(layer, slot, j):
        remote(
            field.at[layer, slot, chunk(j)], field.at[layer, slot, chunk(j)],
            near_send.at[layer, 0], near_recv.at[layer, slot, j], blk=sibling,
        ).wait_recv()

    def add(layer, terms, fresh=False):
        for r in range(0, ROW_TILES, 2):
            result = None if fresh else jnp.concatenate([total[r], total[r + 1]], axis=0)
            for slot, j in terms:
                values = jnp.concatenate(
                    [
                        jnp.concatenate(
                            [tiles[table_ref[slot * 64 + row * 8 + 2 * j + half]] for half in (0, 1)], axis=1
                        )
                        for row in (r, r + 1)
                    ],
                    axis=0,
                )
                product = dot(values, field[layer, slot, chunk(j)])
                result = product if result is None else result + product
            total[r] = result[:TILE]
            total[r + 1] = result[TILE:]

    own_odd, low_odd, high_odd, last_odd = 5 - 2 * core, 3 - 2 * core, 7 - 2 * core, 1 + 6 * core

    def aggregate(layer):
        add(layer, [(4, j) for j in range(CHUNKS)], fresh=True)

        def first_hop(j, carry):
            wait_near(layer, 2, j)
            send_near(layer, 3, j, 2, 0, up)
            send_near(layer, 4, j, 2, 1 + 2 * core, sibling)
            wait_near(layer, 6, j)
            send_near(layer, 5, j, 6, 8, down)
            send_near(layer, 6, j, 6, 5 + 2 * core, sibling)
            wait_near(layer, own_odd, j)
            add(layer, [(own_odd, j), (2, j), (6, j)])
            return carry

        lax.fori_loop(0, CHUNKS, first_hop, 0)
        send_ring(layer)

        def second_hop(j, carry):
            wait_near(layer, 0, j)
            wait_near(layer, 8, j)
            send_near(layer, 7, j, 8 - 8 * core, 7 - 6 * core, sibling)
            wait_near(layer, low_odd, j)
            wait_near(layer, high_odd, j)
            add(layer, [(0, j), (8, j), (low_odd, j), (high_odd, j)])
            return carry

        lax.fori_loop(0, CHUNKS, second_hop, 0)

        def last_hop(j, carry):
            wait_near(layer, last_odd, j)
            return carry

        lax.fori_loop(0, CHUNKS, last_hop, 0)
        add(layer, [(last_odd, j) for j in range(CHUNKS)])
        collect(layer)

    def finish(j):
        near = jnp.concatenate([total[2 * j], total[2 * j + 1]], axis=0)
        return (near + dot(far[chunk(j)], arrived[...])).astype(BF16)

    x_load.wait()
    pick(0)
    pl.semaphore_wait(barrier, (RING - 1) + (GROUPS - 1) + 3)
    send_groups(0)
    for j in range(CHUNKS):
        send_own(0, j)

    tiles_load.wait()
    sums[EMPTY] = jnp.zeros((TILE, TILE), F32)
    tiles[EMPTY] = jnp.zeros((TILE, TILE), BF16)

    def add_earlier(t, carry):
        value = tiles[t].astype(F32) + sums[earlier_ref[t]]
        sums[t] = value
        tiles[t] = value.astype(BF16)
        return carry

    lax.fori_loop(0, EMPTY, add_earlier, 0, unroll=2)

    aggregate(0)
    far_load.wait()

    def exchange(j):
        return remote(pair.at[col, chunk(j)], pair.at[col, chunk(j)], col_send, col_recv.at[j], col=1 - col)

    def finish_first(j, carry):
        pair[col, chunk(j)] = finish(j)
        exchange(j).start()
        return carry

    lax.fori_loop(0, CHUNKS, finish_first, 0)
    w1_load.wait()
    w2_load.wait()
    half = pl.ds(pl.multiple_of(col * WIDTH, WIDTH), WIDTH)

    def project(j, carry):
        remote(
            pair.at[1 - col, chunk(j)], pair.at[1 - col, chunk(j)], col_send, col_recv.at[j], col=1 - col
        ).wait_recv()
        both = jnp.concatenate([pair[0, chunk(j)], pair[1, chunk(j)]], axis=1)
        hidden = jnp.maximum(dot(both, w1[...]), 0.0).astype(BF16)
        field[1, 4, chunk(j)] = dot(hidden, w2[:, half]).astype(BF16)
        send_own(1, j)
        return carry

    lax.fori_loop(0, CHUNKS, project, 0)
    pick(1)
    send_groups(1)
    aggregate(1)

    def finish_second(j, carry):
        out_ref[chunk(j)] = finish(j)
        return carry

    lax.fori_loop(0, CHUNKS, finish_second, 0)

    for layer in range(2):
        for kind in range(8):
            remote(
                field.at[layer, 4], field.at[layer, 4], near_send.at[layer, kind], near_recv.at[layer, 4, 0], blk=sibling
            ).wait_send()
        part = pl.ds(0, GROUPS - 1)
        remote(
            outgoing.at[layer, part], middle.at[layer, part], group_send.at[layer], group_recv.at[layer], blk=sibling
        ).wait_send()
        part = pl.ds(0, RING - 1)
        remote(
            sorted_out.at[layer, part], landed.at[layer, part], ring_send.at[layer], ring_recv.at[layer], blk=sibling
        ).wait_send()
    remote(pair.at[0], pair.at[0], col_send, col_recv.at[0], col=1 - col).wait_send()


def body(
    features, tile_values, tile_index, send_rows, slot_counts, far_weight, weight_one, weight_two
):
    blocks = lax.axis_size("blk")
    position = lax.axis_index("blk")
    capacity = send_rows.shape[2]
    tile_count = tile_values.shape[0]
    offset = (tile_index[0] - position + REACH + blocks) % blocks
    key = offset * 64 + tile_index[2] * ROW_TILES + tile_index[1]
    numbers = jnp.arange(tile_count, dtype=jnp.int32)
    same = (key[:, None] == key[None, :]) & (numbers[:, None] < numbers[None, :])
    earlier = jnp.max(jnp.where(same, numbers[:, None], -1), axis=0)
    earlier = jnp.where(earlier < 0, EMPTY, earlier)
    entries = jnp.arange(SLOTS_NEAR * 64, dtype=jnp.int32)
    table = jnp.max(jnp.where(key[:, None] == entries[None, :], numbers[:, None], -1), axis=0)
    table = jnp.where(table < 0, EMPTY, table)
    live = jnp.arange(capacity, dtype=jnp.int32)[None, :] < slot_counts[0][:, None]
    lists = jnp.where(live, send_rows[0], -1).reshape(ROW_TILES, TILE)

    vmem = pl.BlockSpec(memory_space=pltpu.VMEM)
    smem = pl.BlockSpec(memory_space=pltpu.SMEM)
    hbm = pl.BlockSpec(memory_space=pl.ANY)
    dma = pltpu.SemaphoreType.DMA
    return pl.pallas_call(
        functools.partial(kernel, blocks),
        out_shape=jax.ShapeDtypeStruct((ROWS, WIDTH), BF16),
        in_specs=[smem, smem, vmem, hbm, hbm, hbm, hbm, hbm],
        out_specs=vmem,
        scratch_shapes=[
            pltpu.VMEM((EMPTY + 1, TILE, TILE), BF16),
            pltpu.VMEM((EMPTY + 1, TILE, TILE), F32),
            pltpu.VMEM((ROWS, ROWS), BF16),
            pltpu.VMEM((2 * WIDTH, 2 * WIDTH), BF16),
            pltpu.VMEM((2 * WIDTH, 2 * WIDTH), BF16),
            pltpu.VMEM((2, SLOTS_NEAR, ROWS, WIDTH), BF16),
            pltpu.VMEM((ROW_TILES, TILE, WIDTH), F32),
            pltpu.VMEM((2, ROWS, WIDTH), BF16),
            pltpu.VMEM((ROWS, ROWS), BF16),
            pltpu.VMEM((2, GROUPS, RING * 8, WIDTH), BF16),
            pltpu.VMEM((2, GROUPS, RING * 8, WIDTH), BF16),
            pltpu.VMEM((2, RING, GROUPS * 8, WIDTH), BF16),
            pltpu.VMEM((2, RING, GROUPS * 8, WIDTH), BF16),
            pltpu.VMEM((ROWS, WIDTH), BF16),
            dma((5,)),
            dma((2, 8)),
            dma((2, SLOTS_NEAR, CHUNKS)),
            dma((2,)),
            dma((2,)),
            dma((2,)),
            dma((2,)),
            dma,
            dma((CHUNKS,)),
        ],
        compiler_params=pltpu.CompilerParams(
            collective_id=0, has_side_effects=True, vmem_limit_bytes=56 * 1024 * 1024
        ),
    )(table, earlier, lists, features, tile_values, far_weight, weight_one, weight_two)


def solution(mesh):
    placed = (
        P("blk", "col"),
        P("blk", None, None),
        P(None, "blk"),
        P("blk", None, None),
        P("blk", None),
        P("blk", None),
        P(),
        P(),
    )
    return jax.shard_map(
        body, mesh=mesh, in_specs=placed, out_specs=P("blk", "col"), check_vma=False
    )
```

time: 311 us -> 79.5 us (0.26); the launches traced: 307 us -> 79.3 us
  matrix products: 177 us -> 0 us
  Pallas kernels: 0 us -> 71.6 us
  starting transfers between devices: 66.3 us -> 0 us
  waiting for transfers between devices: 34.7 us -> 0 us
  blocking collectives: 14.7 us -> 0 us
  local copies, waits for them, and re-layouts: 12.6 us -> 3.41 us
  other arithmetic: 0.79 us -> 4.29 us
    dot_general x54 -> x0, matrix products: 177 us -> none  [the longest x16 62.3 us: add_block(): jnp.einsum('rt,tic->ric', place_table, products, precision=lax.Precision....]
    pallas_call x0 -> x1, Pallas kernels: none -> 71.6 us  [body(): pl.pallas_call(functools.partial(kernel, blocks), out_shape=jax.ShapeDtyp...]
    ppermute x16 -> x0, starting transfers between devices: 40.2 us -> none  [from_behind(): return lax.ppermute(block, axis, route)]
    ppermute x16 -> x0, waiting for transfers between devices: 34.7 us -> none  [from_behind(): return lax.ppermute(block, axis, route)]
    all_to_all x2 -> x0, starting transfers between devices: 26.1 us -> none  [aggregate(): lax.all_to_all(outgoing, 'blk', split_axis=0, concat_axis=0, tiled=True)]
    all_gather x2 -> x0, blocking collectives: 14.7 us -> none  [project(): piece = lax.all_gather(aggregated, 'col', axis=1, tiled=True)]
    unnamed x31 -> x3, local copies, waits for them, and re-layouts: 11.8 us -> 2.97 us
  transfers between devices with their start and end apart: 18 -> 0, of which waited for: 4 -> 0; matrix products, arithmetic and copies ran while one was open for 60% -> 0% of each run, Pallas kernels for 0% -> 0%
where the time goes in v1:
time: 79.5 us; the launch traced here: 79.3 us
  Pallas kernels  71.6 us (90%)
  other arithmetic  4.29 us (5%)
  local copies, waits for them, and re-layouts  3.41 us (4%)
    pallas_call x1, Pallas kernels, body(): pl.pallas_call(functools.partial(kernel, blocks), out_shape=jax.ShapeDtyp...  71.6 us
    unnamed x3, local copies, waits for them, and re-layouts  2.97 us

profile of v1, /device:TPU:1, one launch (start us, length us, event | category | flops | bytes accessed | tf_op | source)
XLA Modules:
  0.0 79.3 jit_solution(7205099377217081331)
XLA Ops:
  0.0 0.5 broadcast.76
  0.5 1.3 %reduce.11 = s32[128]{0:T(128)S(1)} reduce(s32[1,128]{1,0:T(1,128)} %param.12, s32[]{:T(128)} %broadcast.76), dimensions={0}, to_apply=%param.12.reduce_sub_computation.3 | reduce | bytes 1028 | tf_op args[4]
  1.8 0.1 lt.67
  1.9 0.8 %fusion.9 = (s32[288]{0:T(512)S(1)}, s32[288]{0:T(512)S(1)}, s32[288]{0:T(512)S(1)}, s32[288]{0:T(512)S(1)}) fusion(s32[3,288]{1,0:T(4,128)} %param.10, s32[]{:T(128)S(6)} %axis_index.15), kind=kLoop, calls=%fused_computation.24 | loop fusion | flops 4896 | bytes 8068 | tf_op jit(solution)/shard_map/add | solution.py:279
  2.8 0.2 select_reduce_fusion.1
  2.9 0.6 compare_select_fusion.3.earlier_ref
  3.5 0.2 select_reduce_fusion
  3.7 0.6 compare_select_fusion.table_ref
  4.3 0.1 lt.65
  4.4 0.1 lt.68
  4.5 0.1 lt.69
  4.6 0.8 copy.11
  5.4 0.1 squeeze.9
  5.5 0.6 compare_select_fusion.4.lists_ref
  6.1 71.6 %shard_map.82 = bf16[1024,128]{1,0:T(8,128)(2,1)} custom-call(s32[576]{0:T(1024)} %compare_select_fusion.table_ref, s32[288]{0:T(512)} %compare_select_fusion.3.earlier_ref, s32[8,128]{1,0:T(8,128)} %compare_select_fusion.4.lists_ref, bf16[1024,128]{1,0:T(8,128)(2,1)} %x_hbm.1, bf16[288,128,128]{2,1,0:T(8,128)(2,1)} %tiles_hbm.1, ...), custom_call_target="tpu_custom_call" | custom-call | tf_op jit(solution)/shard_map/pallas_call | solution.py:294
  77.7 1.7 %copy.13 = bf16[1024,128]{1,0:T(8,128)(2,1)} copy(bf16[1024,128]{1,0:T(8,128)(2,1)} %shard_map.82) | data formatting | bytes 524288
  (2 shorter events, 0.0 us)

commit v2 on v1

--- a/solution.py
+++ b/solution.py
@@ -28,8 +28,8 @@
 
 
 def kernel(
-    blocks, table_ref, earlier_ref, lists_ref, x_hbm, tiles_hbm, far_hbm, w1_hbm, w2_hbm, out_ref,
-    tiles, sums, far, w1, w2, field, total, pair, picks, outgoing, middle, sorted_out, landed, arrived,
+    blocks, index_ref, lists_ref, counts_ref, x_hbm, tiles_hbm, far_hbm, w1_hbm, w2_hbm, out_ref,
+    keys, plan_vmem, plan, tiles, sums, far, w1, w2, field, total, pair, picks, outgoing, middle, sorted_out, landed, arrived,
     load_sem, near_send, near_recv, group_send, group_recv, ring_send, ring_recv, col_send, col_recv,
 ):
     blk = lax.axis_index("blk")
@@ -41,6 +41,7 @@
     place = lax.rem(blk, RING)
     ring_base = blk - place
     group = blk // RING
+    height = place // 2
 
     x_load = pltpu.make_async_copy(x_hbm, field.at[0, 4], load_sem.at[0])
     tiles_load = pltpu.make_async_copy(tiles_hbm, tiles.at[pl.ds(0, EMPTY)], load_sem.at[1])
@@ -71,13 +72,54 @@
             src_ref=src, dst_ref=dst, send_sem=send, recv_sem=recv, device_id=device, device_id_type=MESH
         )
 
-    for a in range(ROW_TILES):
-        column = jnp.broadcast_to(lists_ref[a : a + 1, :], (TILE, TILE)).T
-        for b in range(ROW_TILES):
-            numbers = lax.broadcasted_iota(jnp.int32, (TILE, TILE), 1) + b * TILE
-            picks[a * TILE : (a + 1) * TILE, b * TILE : (b + 1) * TILE] = jnp.where(
-                column == numbers, 1.0, 0.0
-            ).astype(BF16)
+    offset = index_ref[0:1, :] - blk + REACH
+    offset = jnp.where(offset < 0, offset + blocks, offset)
+    offset = jnp.where(offset >= blocks, offset - blocks, offset)
+    keys[...] = jnp.full(keys.shape, -1, jnp.int32)
+    keys[0:1, 0:EMPTY] = offset * 64 + index_ref[2:3, :] * ROW_TILES + index_ref[1:2, :]
+    across = lax.broadcasted_iota(jnp.int32, (TILE, TILE), 1)
+    along = lax.broadcasted_iota(jnp.int32, (TILE, TILE), 0)
+    rows = [jnp.broadcast_to(keys[0:1, b * TILE : (b + 1) * TILE], (TILE, TILE)) for b in range(3)]
+    columns = [row.T for row in rows]
+
+    def last(hits):
+        best = None
+        for b, hit in hits:
+            found = jnp.max(jnp.where(hit, along + b * TILE, -1), axis=0, keepdims=True)
+            best = found if best is None else jnp.maximum(best, found)
+        return jnp.where(best < 0, EMPTY, best)
+
+    for g in range(5):
+        plan_vmem[g : g + 1, :] = last([(b, columns[b] == across + g * TILE) for b in range(3)])
+    for g in range(3):
+        plan_vmem[5 + g : 6 + g, :] = last(
+            [
+                (b, (columns[b] == rows[g]) & (along < across) if b == g else columns[b] == rows[g])
+                for b in range(g + 1)
+            ]
+        )
+    plan_load = pltpu.make_async_copy(plan_vmem, plan, load_sem.at[5])
+    plan_load.start()
+
+    live = lax.broadcasted_iota(jnp.int32, (8, TILE), 0) < counts_ref[...]
+    lists = jnp.where(live, lists_ref[...], -1)
+    eight = lax.broadcasted_iota(jnp.int32, (8, TILE), 1)
+
+    def mark(a, carry):
+        turned = pltpu.roll(lists, lax.rem(TILE - 16 * a, TILE), 1)
+        for k in range(0, 16, 2):
+            first = jnp.broadcast_to(turned[:, k : k + 1], (8, TILE))
+            second = jnp.broadcast_to(turned[:, k + 1 : k + 2], (8, TILE))
+            for b in range(ROW_TILES):
+                numbers = eight + b * TILE
+                pairs = jnp.concatenate(
+                    [jnp.where(first == numbers, 1.0, 0.0), jnp.where(second == numbers, 1.0, 0.0)], axis=0
+                )
+                start = pl.multiple_of(a * TILE + k * 8, 16)
+                picks[pl.ds(start, 16), b * TILE : (b + 1) * TILE] = pairs.astype(BF16)
+        return carry
+
+    lax.fori_loop(0, ROW_TILES, mark, 0)
 
     def pick(layer):
         for a in range(CHUNKS):
@@ -143,7 +185,8 @@
                 values = jnp.concatenate(
                     [
                         jnp.concatenate(
-                            [tiles[table_ref[slot * 64 + row * 8 + 2 * j + half]] for half in (0, 1)], axis=1
+                            [tiles[plan[slot // 2, slot % 2 * 64 + row * 8 + 2 * j + half]] for half in (0, 1)],
+                            axis=1,
                         )
                         for row in (r, r + 1)
                     ],
@@ -171,7 +214,6 @@
             return carry
 
         lax.fori_loop(0, CHUNKS, first_hop, 0)
-        send_ring(layer)
 
         def second_hop(j, carry):
             wait_near(layer, 0, j)
@@ -182,7 +224,9 @@
             add(layer, [(0, j), (8, j), (low_odd, j), (high_odd, j)])
             return carry
 
-        lax.fori_loop(0, CHUNKS, second_hop, 0)
+        lax.fori_loop(0, CHUNKS // 2, second_hop, 0)
+        send_ring(layer)
+        lax.fori_loop(CHUNKS // 2, CHUNKS, second_hop, 0)
 
         def last_hop(j, carry):
             wait_near(layer, last_odd, j)
@@ -199,16 +243,17 @@
     x_load.wait()
     pick(0)
     pl.semaphore_wait(barrier, (RING - 1) + (GROUPS - 1) + 3)
-    send_groups(0)
     for j in range(CHUNKS):
         send_own(0, j)
-
+    send_groups(0)
+
+    plan_load.wait()
     tiles_load.wait()
     sums[EMPTY] = jnp.zeros((TILE, TILE), F32)
     tiles[EMPTY] = jnp.zeros((TILE, TILE), BF16)
 
     def add_earlier(t, carry):
-        value = tiles[t].astype(F32) + sums[earlier_ref[t]]
+        value = tiles[t].astype(F32) + sums[plan[5 + t // TILE, t % TILE]]
         sums[t] = value
         tiles[t] = value.astype(BF16)
         return carry
@@ -238,10 +283,30 @@
         both = jnp.concatenate([pair[0, chunk(j)], pair[1, chunk(j)]], axis=1)
         hidden = jnp.maximum(dot(both, w1[...]), 0.0).astype(BF16)
         field[1, 4, chunk(j)] = dot(hidden, w2[:, half]).astype(BF16)
-        send_own(1, j)
+        send_near(1, 2, j, 4, 3 + 2 * core, sibling)
+
+        @pl.when(height != GROUPS - 1)
+        def _():
+            send_near(1, 0, j, 4, 2, up)
+
+        @pl.when(height != 0)
+        def _():
+            send_near(1, 1, j, 4, 6, down)
+
         return carry
 
     lax.fori_loop(0, CHUNKS, project, 0)
+
+    @pl.when(height == GROUPS - 1)
+    def _():
+        for j in range(CHUNKS):
+            send_near(1, 0, j, 4, 2, up)
+
+    @pl.when(height == 0)
+    def _():
+        for j in range(CHUNKS):
+            send_near(1, 1, j, 4, 6, down)
+
     pick(1)
     send_groups(1)
     aggregate(1)
@@ -272,31 +337,18 @@
     features, tile_values, tile_index, send_rows, slot_counts, far_weight, weight_one, weight_two
 ):
     blocks = lax.axis_size("blk")
-    position = lax.axis_index("blk")
-    capacity = send_rows.shape[2]
-    tile_count = tile_values.shape[0]
-    offset = (tile_index[0] - position + REACH + blocks) % blocks
-    key = offset * 64 + tile_index[2] * ROW_TILES + tile_index[1]
-    numbers = jnp.arange(tile_count, dtype=jnp.int32)
-    same = (key[:, None] == key[None, :]) & (numbers[:, None] < numbers[None, :])
-    earlier = jnp.max(jnp.where(same, numbers[:, None], -1), axis=0)
-    earlier = jnp.where(earlier < 0, EMPTY, earlier)
-    entries = jnp.arange(SLOTS_NEAR * 64, dtype=jnp.int32)
-    table = jnp.max(jnp.where(key[:, None] == entries[None, :], numbers[:, None], -1), axis=0)
-    table = jnp.where(table < 0, EMPTY, table)
-    live = jnp.arange(capacity, dtype=jnp.int32)[None, :] < slot_counts[0][:, None]
-    lists = jnp.where(live, send_rows[0], -1).reshape(ROW_TILES, TILE)
-
     vmem = pl.BlockSpec(memory_space=pltpu.VMEM)
-    smem = pl.BlockSpec(memory_space=pltpu.SMEM)
     hbm = pl.BlockSpec(memory_space=pl.ANY)
     dma = pltpu.SemaphoreType.DMA
     return pl.pallas_call(
         functools.partial(kernel, blocks),
-        out_shape=jax.ShapeDtypeStruct((ROWS, WIDTH), BF16),
-        in_specs=[smem, smem, vmem, hbm, hbm, hbm, hbm, hbm],
+        out_shape=pltpu.VMEM((ROWS, WIDTH), BF16),
+        in_specs=[vmem, vmem, vmem, hbm, hbm, hbm, hbm, hbm],
         out_specs=vmem,
         scratch_shapes=[
+            pltpu.VMEM((8, 3 * TILE), jnp.int32),
+            pltpu.VMEM((8, TILE), jnp.int32),
+            pltpu.SMEM((8, TILE), jnp.int32),
             pltpu.VMEM((EMPTY + 1, TILE, TILE), BF16),
             pltpu.VMEM((EMPTY + 1, TILE, TILE), F32),
             pltpu.VMEM((ROWS, ROWS), BF16),
@@ -311,7 +363,7 @@
             pltpu.VMEM((2, RING, GROUPS * 8, WIDTH), BF16),
             pltpu.VMEM((2, RING, GROUPS * 8, WIDTH), BF16),
             pltpu.VMEM((ROWS, WIDTH), BF16),
-            dma((5,)),
+            dma((6,)),
             dma((2, 8)),
             dma((2, SLOTS_NEAR, CHUNKS)),
             dma((2,)),
@@ -324,7 +376,10 @@
         compiler_params=pltpu.CompilerParams(
             collective_id=0, has_side_effects=True, vmem_limit_bytes=56 * 1024 * 1024
         ),
-    )(table, earlier, lists, features, tile_values, far_weight, weight_one, weight_two)
+    )(
+        tile_index, jnp.swapaxes(send_rows, 1, 2)[0], slot_counts,
+        features, tile_values, far_weight, weight_one, weight_two,
+    )
 
 
 def solution(mesh):

time: 79.5 us -> 65.8 us (0.83)
  Pallas kernels: 71.6 us -> 64.9 us
  other arithmetic: 4.29 us -> 0 us
  local copies, waits for them, and re-layouts: 3.41 us -> 0.71 us
    pallas_call x1, Pallas kernels: 71.6 us -> 64.9 us  [body(): pl.pallas_call(functools.partial(kernel, blocks), out_shape=pltpu.VMEM((R...]
    unnamed x3 -> x1, local copies, waits for them, and re-layouts: 2.97 us -> 0.71 us
    select_n x3 -> x0, other arithmetic: 1.78 us -> none  [the longest x1 0.6 us: body(): table = jnp.where(table < 0, EMPTY, table)]
    unnamed x1 -> x0, other arithmetic: 1.32 us -> none
    add x2 -> x0, other arithmetic: 0.85 us -> none  [body(): key = offset * 64 + tile_index[2] * ROW_TILES + tile_index[1]]
where the time goes in v2:
time: 65.8 us; the launch traced here: 65.7 us
  Pallas kernels  64.9 us (99%)
  local copies, waits for them, and re-layouts  0.71 us (1%)
    pallas_call x1, Pallas kernels, body(): pl.pallas_call(functools.partial(kernel, blocks), out_shape=pltpu.VMEM((R...  64.9 us

profile of v2, /device:TPU:1, one launch (start us, length us, event | category | flops | bytes accessed | tf_op | source)
XLA Modules:
  0.0 65.7 jit_solution(7573780846442774460)
XLA Ops:
  0.0 64.9 %shard_map.82 = bf16[1024,128]{1,0:T(8,128)(2,1)S(1)} custom-call(s32[3,288]{1,0:T(4,128)} %index_ref.1, s32[8,128]{1,0:T(8,128)} %bitcast.3, s32[1,128]{1,0:T(1,128)} %counts_ref.1, bf16[1024,128]{1,0:T(8,128)(2,1)} %x_hbm.1, bf16[288,128,128]{2,1,0:T(8,128)(2,1)} %tiles_hbm.1, bf16[1024,1024]{1,0:T(8,128)(2,1)} %far_hbm.1, bf16[256,256]{1,0:T(8,128)(2,1)} %w1_hbm.1, ...), custom_call_target="tpu_custom_call" | custom-call | tf_op jit(solution)/shard_map/pallas_call | solution.py:343
  65.0 0.7 %copy.10 = bf16[1024,128]{1,0:T(8,128)(2,1)} copy(bf16[1024,128]{1,0:T(8,128)(2,1)S(1)} %shard_map.82) | data formatting | bytes 524288

commit v3 on v2

--- a/solution.py
+++ b/solution.py
@@ -21,6 +21,7 @@
 RING = 16
 GROUPS = 8
 EMPTY = 288
+RING_AFTER = (3, 2)
 
 
 def dot(a, b):
@@ -224,16 +225,16 @@
             add(layer, [(0, j), (8, j), (low_odd, j), (high_odd, j)])
             return carry
 
-        lax.fori_loop(0, CHUNKS // 2, second_hop, 0)
+        lax.fori_loop(0, RING_AFTER[layer], second_hop, 0)
         send_ring(layer)
-        lax.fori_loop(CHUNKS // 2, CHUNKS, second_hop, 0)
+        lax.fori_loop(RING_AFTER[layer], CHUNKS, second_hop, 0)
 
         def last_hop(j, carry):
             wait_near(layer, last_odd, j)
+            add(layer, [(last_odd, j)])
             return carry
 
         lax.fori_loop(0, CHUNKS, last_hop, 0)
-        add(layer, [(last_odd, j) for j in range(CHUNKS)])
         collect(layer)
 
     def finish(j):
@@ -271,7 +272,8 @@
         exchange(j).start()
         return carry
 
-    lax.fori_loop(0, CHUNKS, finish_first, 0)
+    for j in range(CHUNKS):
+        finish_first(j, 0)
     w1_load.wait()
     w2_load.wait()
     half = pl.ds(pl.multiple_of(col * WIDTH, WIDTH), WIDTH)
@@ -315,7 +317,8 @@
         out_ref[chunk(j)] = finish(j)
         return carry
 
-    lax.fori_loop(0, CHUNKS, finish_second, 0)
+    for j in range(CHUNKS):
+        finish_second(j, 0)
 
     for layer in range(2):
         for kind in range(8):

time: 65.8 us -> 64.2 us (0.976)
  Pallas kernels: 64.9 us -> 63.4 us
    pallas_call x1, Pallas kernels: 64.9 us -> 63.4 us  [body(): pl.pallas_call(functools.partial(kernel, blocks), out_shape=pltpu.VMEM((R...]
where the time goes in v3:
time: 64.2 us; the launch traced here: 64.1 us
  Pallas kernels  63.4 us (99%)
  local copies, waits for them, and re-layouts  0.71 us (1%)
    pallas_call x1, Pallas kernels, body(): pl.pallas_call(functools.partial(kernel, blocks), out_shape=pltpu.VMEM((R...  63.4 us

profile of v3, /device:TPU:1, one launch (start us, length us, event | category | flops | bytes accessed | tf_op | source)
XLA Modules:
  0.0 64.1 jit_solution(6239670960680241461)
XLA Ops:
  0.0 63.4 %shard_map.82 = bf16[1024,128]{1,0:T(8,128)(2,1)S(1)} custom-call(s32[3,288]{1,0:T(4,128)} %index_ref.1, s32[8,128]{1,0:T(8,128)} %bitcast.3, s32[1,128]{1,0:T(1,128)} %counts_ref.1, bf16[1024,128]{1,0:T(8,128)(2,1)} %x_hbm.1, bf16[288,128,128]{2,1,0:T(8,128)(2,1)} %tiles_hbm.1, bf16[1024,1024]{1,0:T(8,128)(2,1)} %far_hbm.1, bf16[256,256]{1,0:T(8,128)(2,1)} %w1_hbm.1, ...), custom_call_target="tpu_custom_call" | custom-call | tf_op jit(solution)/shard_map/pallas_call | solution.py:346
  63.4 0.7 %copy.10 = bf16[1024,128]{1,0:T(8,128)(2,1)} copy(bf16[1024,128]{1,0:T(8,128)(2,1)S(1)} %shard_map.82) | data formatting | bytes 524288
